TPU v7x, 32 devices: a whole 2x2x4 slice. The times are simulated.
32 devices in a mesh: graph: 16 (over z, y, x), rep: 2 (over core).
Axes of the slice: x: 2, y: 2, z: 4, core: 2. Of those that a mesh axis runs over, the one named last changes fastest.
Arguments:
- grad_out: bfloat16 [8192, 256], P(('graph', 'rep')), may hold values from -6 to 6
- pre_act: bfloat16 [8192, 256], P(('graph', 'rep')), may hold values from -6 to 6
- aggregated: bfloat16 [8192, 256], P(('graph', 'rep')), may hold values from -0.3125 to 0.3125
- weight: bfloat16 [256, 256], replicated, may hold values from -0.375 to 0.375
- adj_tiles: bfloat16 [16, 2, 16, 2, 128, 128], P('graph', 'rep'), may hold values from 0 to 0.039794922
- tile_row: int32 [16, 2, 16, 2], P('graph', 'rep'), may hold values from 0 to 1
- tile_col: int32 [16, 2, 16, 2], P('graph', 'rep'), may hold values from 0 to 3
- tile_count: int32 [16, 2, 16], P('graph', 'rep'), may hold values from 0 to 2, as said below
- node_perm: int32 [16, 512], P('graph'), may hold values from 0 to 511, each once within a row
Outputs:
- input_grad: bfloat16 [8192, 256], P(('graph', 'rep'))
- weight_grad: float32 [256, 256], replicated
- relu_grad: bfloat16 [8192, 256], P(('graph', 'rep'))
Inputs may be any that keep to these rules, and one draw needn't show every extreme that they name: tile_count[g, r, g] is 2 for every partition g and replica r. `node_perm`: each row is a permutation.
All inputs are finite; a program needn't handle non-finite values.
Results may differ from a plain program's by a relative error of at most 0.0049.
Values may be sent and summed in bfloat16 or wider, within the bound.
A program may use at most 128 MiB of HBM per device.

v0:
```python
import jax
import jax.numpy as jnp
from jax import lax
from jax.sharding import PartitionSpec as P


def tile_products(running, sources, row_count, local_tiles, local_row, local_col, local_count):
    piece_parts = sources.shape[0] // row_count
    tile_size = local_tiles.shape[-1]
    feature_width = sources.shape[1]
    blocks = sources.reshape(piece_parts, row_count // tile_size, tile_size, feature_width)
    part_index = jnp.arange(piece_parts, dtype=jnp.int32)
    for slot_index in range(local_tiles.shape[1]):
        chosen = blocks[part_index, local_row[:, slot_index]]
        product = jnp.einsum(
            "kab,kac->kbc", local_tiles[:, slot_index], chosen, preferred_element_type=jnp.float32
        )
        alive = (local_count > slot_index).astype(jnp.float32)
        running = running.at[local_col[:, slot_index]].add(product * alive[:, None, None])
    return running


def body(
    grad_out, pre_act, aggregated, weight, adj_tiles, tile_row, tile_col, tile_count, node_perm
):
    row_count = grad_out.shape[0]
    feature_width = weight.shape[0]
    relu_grad = jnp.where(pre_act > 0, grad_out, jnp.zeros_like(grad_out))
    partial_weight = lax.dot_general(
        aggregated, relu_grad, (((0,), (0,)), ((), ())), preferred_element_type=jnp.float32
    )
    local_tiles = adj_tiles[0, 0]
    local_row = tile_row[0, 0]
    local_col = tile_col[0, 0]
    local_count = tile_count[0, 0]
    local_perm = node_perm[0]
    tile_size = local_tiles.shape[-1]
    col_blocks = lax.axis_size("rep") * (row_count // tile_size)
    empty = jnp.zeros((col_blocks, tile_size, feature_width), jnp.float32)
    back_agg = lax.dot_general(
        relu_grad, weight, (((1,), (1,)), ((), ())), preferred_element_type=jnp.float32
    ).astype(jnp.bfloat16)
    running = tile_products(
        empty,
        lax.all_gather(back_agg, "graph", axis=0, tiled=True),
        row_count,
        local_tiles,
        local_row,
        local_col,
        local_count,
    )
    partial_grad = running.reshape(col_blocks * tile_size, feature_width)
    input_grad = lax.psum_scatter(
        jnp.take(partial_grad, local_perm, axis=0), "rep", scatter_dimension=0, tiled=True
    ).astype(jnp.bfloat16)
    weight_grad = lax.psum(partial_weight, ("graph", "rep"))
    return (input_grad, weight_grad, relu_grad)


def solution(mesh):
    placed = (
        P(("graph", "rep"), None),
        P(("graph", "rep"), None),
        P(("graph", "rep"), None),
        P(),
        P("graph", "rep", None, None, None, None),
        P("graph", "rep", None, None),
        P("graph", "rep", None, None),
        P("graph", "rep", None),
        P("graph", None),
    )
    return jax.shard_map(
        body,
        mesh=mesh,
        in_specs=placed,
        out_specs=(P(("graph", "rep"), None), P(), P(("graph", "rep"), None)),
        check_vma=False,
    )
```

profile of v0, /device:TPU:0, one launch (start us, length us, event | category | flops | bytes accessed | tf_op | source)
XLA Modules:
  0.0 160.9 jit_solution(16786216906860122379)
XLA Ops:
  8.0 0.0 copy-start
  8.0 0.0 copy-start.2
  8.0 0.0 all-gather.2.cloned.1.call-start
  8.1 1.1 compare_select_fusion
  9.1 0.0 copy-done
  9.2 0.0 copy-start.1
  9.2 0.9 convolution_convert_fusion
  10.0 0.0 all-gather.2.cloned.1.call-update
  10.1 0.0 all-reduce.2.cloned.1.call-start
  10.1 1.8 %convolution_bitcast_fusion = f32[256,256]{0,1:T(8,128)} fusion(bf16[256,256]{1,0:T(8,128)(2,1)S(1)} %compare_select_fusion, bf16[256,256]{1,0:T(8,128)(2,1)} %param.11), kind=kOutput, calls=%fused_computation.7 | convolution fusion | flops 33554432 | bytes 524288 | tf_op jit(solution)/shard_map/dot_general | solution.py:29
  12.0 0.0 all-reduce.2.cloned.1.call-update
  12.0 0.0 reduce-scatter.2.cloned.1.call-start
  12.0 0.7 compare_select_fusion.1
  12.7 0.7 compare_and_fusion
  13.4 0.8 fusion.10
  14.2 0.8 fusion.6
  14.9 0.7 fusion.1
  15.6 0.0 copy-done.2
  15.6 0.1 copy.25
  15.7 60.0 %all-gather.2.cloned.1.call-done = bf16[4096,256]{1,0:T(8,128)(2,1)} async-done(((bf16[256,256]{1,0:T(8,128)(2,1)}), bf16[4096,256]{1,0:T(8,128)(2,1)}) %all-gather.2.cloned.1.call-update) | async-done | bytes 2097168 | tf_op jit(solution)/shard_map/all_gather | solution.py:45
  75.7 3.2 %gather_fusion.1 = bf16[16,128,256]{2,1,0:T(8,128)(2,1)} fusion(bf16[16,2,128,256]{3,2,1,0:T(8,128)(2,1)} %bitcast.44, s32[16]{0:T(128)S(1)} %get-tuple-element.9), kind=kCustom, calls=%fused_computation.1 | custom fusion | bytes 2097280 | tf_op jit(solution)/shard_map/gather | solution.py:14
  78.9 0.0 copy-done.1
  78.9 2.2 %gather_fusion = bf16[16,128,256]{2,1,0:T(8,128)(2,1)S(1)} fusion(bf16[16,2,128,256]{3,2,1,0:T(8,128)(2,1)} %bitcast.45, s32[16]{0:T(128)S(1)} %get-tuple-element.10), kind=kCustom, calls=%fused_computation | custom fusion | bytes 2097280 | tf_op jit(solution)/shard_map/gather | solution.py:14
  81.1 1.8 %multiply_bitcast_fusion.1 = f32[16,128,256]{1,2,0:T(8,128)} fusion(bf16[16,128,256]{2,1,0:T(8,128)(2,1)S(1)} %gather_fusion, f32[16]{0:T(128)S(1)} %get-tuple-element.14, bf16[16,2,128,128]{3,2,0,1:T(8,128)(2,1)S(1)} %bitcast.42), kind=kOutput, calls=%fused_computation.6 | convolution fusion | flops 134742016 | bytes 3670528 | tf_op jit(solution)/shard_map/kab,kac->kbc/dot_general | solution.py:15
  83.0 1.9 %copy.18 = f32[16,128,256]{2,1,0:T(8,128)S(1)} copy(f32[16,128,256]{1,2,0:T(8,128)} %multiply_bitcast_fusion.1) | data formatting | bytes 4194304 | tf_op jit(solution)/shard_map/mul | solution.py:19
  84.9 3.1 %multiply_bitcast_fusion = f32[16,128,256]{1,2,0:T(8,128)} fusion(bf16[16,128,256]{2,1,0:T(8,128)(2,1)} %gather_fusion.1, f32[16]{0:T(128)S(1)} %get-tuple-element.13, bf16[16,2,128,128]{3,2,0,1:T(8,128)(2,1)S(1)} %bitcast.43), kind=kOutput, calls=%fused_computation.5 | convolution fusion | flops 134742016 | bytes 3670528 | tf_op jit(solution)/shard_map/kab,kac->kbc/dot_general | solution.py:15
  88.0 2.9 %copy.20 = f32[16,128,256]{2,1,0:T(8,128)} copy(f32[16,128,256]{1,2,0:T(8,128)} %multiply_bitcast_fusion) | data formatting | bytes 4194304 | tf_op jit(solution)/shard_map/mul | solution.py:19
  90.9 2.2 %scatter_fusion = f32[4,128,256]{2,1,0:T(8,128)S(1)} fusion(f32[4,128,256]{2,1,0:T(8,128)S(1)} %broadcast_in_dim.10, s32[16]{0:T(128)S(1)} %get-tuple-element.12, f32[16,128,256]{2,1,0:T(8,128)S(1)} %copy.18), kind=kCustom, calls=%fused_computation.3 | custom fusion | flops 524288 | bytes 6291520 | tf_op jit(solution)/shard_map/scatter-add | solution.py:19
  93.1 3.5 %scatter_fusion.1 = f32[4,128,256]{2,1,0:T(8,128)S(1)} fusion(f32[4,128,256]{2,1,0:T(8,128)S(1)} %scatter_fusion, s32[16]{0:T(128)S(1)} %get-tuple-element.11, f32[16,128,256]{2,1,0:T(8,128)} %copy.20), kind=kCustom, calls=%fused_computation.4 | custom fusion | flops 524288 | bytes 6291520 | tf_op jit(solution)/shard_map/scatter-add | solution.py:19
  96.6 1.6 gather_fusion.2
  98.2 0.9 broadcast_select_fusion
  99.1 0.0 reduce-scatter.2.cloned.1.call-update
  99.1 51.0 %all-reduce.2.cloned.1.call-done = f32[256,256]{0,1:T(8,128)} async-done(((f32[256,256]{0,1:T(8,128)}), f32[256,256]{0,1:T(8,128)}) %all-reduce.2.cloned.1.call-update) | async-done | bytes 262160 | tf_op jit(solution)/shard_map/psum | solution.py:56
  150.1 1.8 %copy.21 = f32[256,256]{1,0:T(8,128)} copy(f32[256,256]{0,1:T(8,128)} %all-reduce.2.cloned.1.call-done) | data formatting | bytes 524288
  151.9 0.0 reduce-scatter.2.cloned.1.call-done
  151.9 1.6 %convert_element_type.31 = bf16[256,256]{1,0:T(8,128)(2,1)} convert(f32[256,256]{1,0:T(8,128)} %reduce-scatter.2.cloned.1.call-done) | non-fusion elementwise | flops 65536 | bytes 393216 | tf_op jit(solution)/shard_map/convert_element_type | solution.py:55
  (2 shorter events, 0.0 us)
Async XLA Ops:
  8.0 1.1 copy-start
  8.0 7.6 %copy-start.2 = (bf16[1,1,16,2,128,128]{5,4,3,2,1,0:T(8,128)(2,1)S(1)}, bf16[1,1,16,2,128,128]{5,4,3,2,1,0:T(8,128)(2,1)}, u32[]{:S(2)}) copy-start(bf16[1,1,16,2,128,128]{5,4,3,2,1,0:T(8,128)(2,1)} %param.13) | copy-start | bytes 3145732
  8.0 67.7 %all-gather.2.cloned.1.call-start = ((), (), s32[]{:S(2)}) async-start(), calls=%async_computation.1 | async-start | bytes 2228224 | tf_op jit(solution)/shard_map/all_gather | solution.py:45
  9.2 69.8 %copy-start.1 = (bf16[256,256]{1,0:T(8,128)(2,1)}, bf16[256,256]{1,0:T(8,128)(2,1)S(1)}, u32[]{:S(2)}) copy-start(bf16[256,256]{1,0:T(8,128)(2,1)S(1)} %compare_select_fusion) | copy-start | bytes 393220
  10.1 140.0 %all-reduce.2.cloned.1.call-start = ((), (), s32[]{:S(2)}) async-start(), calls=%async_computation.3 | async-start | bytes 524288 | tf_op jit(solution)/shard_map/psum | solution.py:56
  12.0 139.9 %reduce-scatter.2.cloned.1.call-start = ((), (), s32[]{:S(2)}) async-start(), calls=%async_computation.2 | async-start | bytes 786432 | tf_op jit(solution)/shard_map/reduce_scatter | solution.py:53
Sparse Core Ops, SparseCore 0:
  12.2 63.4 all-gather.1
  99.3 6.6 reduce-scatter.1
Sparse Core Ops, SparseCore 1:
  17.5 132.5 all-reduce.1
where the time goes:
time: 161 us
  waiting for transfers between devices  111 us (69%)
  between operations  15.6 us (10%)
  local copies, waits for them, and re-layouts  13.7 us (9%)
  other arithmetic  12.8 us (8%)
  matrix products  7.62 us (5%)
    all_gather x1, waiting for transfers between devices, body(): lax.all_gather(back_agg, 'graph', axis=0, tiled=True)  60 us
    psum x1, waiting for transfers between devices, body(): weight_grad = lax.psum(partial_weight, ('graph', 'rep'))  51 us
    scatter-add x2, other arithmetic, tile_products(): running.at[local_col[:, slot_index]].add(product * alive[:, None, None])  5.67 us
    gather x2, local copies, waits for them, and re-layouts, tile_products(): chosen = blocks[part_index, local_row[:, slot_index]]  5.41 us
    dot_general x2, matrix products, tile_products(): jnp.einsum('kab,kac->kbc', local_tiles[:, slot_index], chosen, preferred_...  4.91 us
    mul x2, local copies, waits for them, and re-layouts, tile_products(): product * alive[:, None, None]  4.82 us
  transfers between devices with their start and end apart: 3, of which 2 were waited for; matrix products, arithmetic and copies ran while one was open for 19% of the time, Pallas kernels for 0%

commit v1 on v0

--- a/solution.py
+++ b/solution.py
@@ -53,7 +53,8 @@
     input_grad = lax.psum_scatter(
         jnp.take(partial_grad, local_perm, axis=0), "rep", scatter_dimension=0, tiled=True
     ).astype(jnp.bfloat16)
-    weight_grad = lax.psum(partial_weight, ("graph", "rep"))
+    one_axis = lax.psum(partial_weight, "rep")
+    weight_grad = lax.psum(one_axis, "graph")
     return (input_grad, weight_grad, relu_grad)
 
 

time: 161 us -> 199 us (1.24)
  waiting for transfers between devices: 111 us -> 156 us
  other arithmetic: 12.8 us -> 9.33 us
  matrix products: 7.62 us -> 5.07 us
    psum x1 -> x2, waiting for transfers between devices: 51 us -> 111 us  [the longest x1 90.3 us: body(): weight_grad = lax.psum(one_axis, 'graph')]
    all_gather x1, waiting for transfers between devices: 60 us -> 44.9 us  [body(): lax.all_gather(back_agg, 'graph', axis=0, tiled=True)]
    dot_general x2, matrix products: 4.91 us -> 2.36 us  [tile_products(): jnp.einsum('kab,kac->kbc', local_tiles[:, slot_index], chosen, preferred_...]
  transfers between devices with their start and end apart: 3 -> 4, of which waited for: 2 -> 3; matrix products, arithmetic and copies ran while one was open for 19% -> 12% of each run, Pallas kernels for 0% -> 0%
where the time goes in v1:
time: 199 us
  waiting for transfers between devices  156 us (78%)
  between operations  15.7 us (8%)
  local copies, waits for them, and re-layouts  12.7 us (6%)
  other arithmetic  9.33 us (5%)
  matrix products  5.07 us (3%)
    psum x1, waiting for transfers between devices, body(): weight_grad = lax.psum(one_axis, 'graph')  90.3 us
    all_gather x1, waiting for transfers between devices, body(): lax.all_gather(back_agg, 'graph', axis=0, tiled=True)  44.9 us
    psum x1, waiting for transfers between devices, body(): one_axis = lax.psum(partial_weight, 'rep')  20.5 us
    scatter-add x2, other arithmetic, tile_products(): running.at[local_col[:, slot_index]].add(product * alive[:, None, None])  5.66 us
    gather x2, local copies, waits for them, and re-layouts, tile_products(): chosen = blocks[part_index, local_row[:, slot_index]]  5.39 us
  transfers between devices with their start and end apart: 4, of which 3 were waited for; matrix products, arithmetic and copies ran while one was open for 12% of the time, Pallas kernels for 0%

profile of v1, /device:TPU:0, one launch (start us, length us, event | category | flops | bytes accessed | tf_op | source)
XLA Modules:
  0.0 198.7 jit_solution(11421232762565708792)
XLA Ops:
  8.0 0.0 copy-start
  8.0 0.0 copy-start.3
  8.0 0.0 copy-start.4
  8.0 0.0 copy-start.7
  8.0 0.0 copy-start.5
  8.1 0.0 copy-start.6
  8.1 0.0 all-reduce.3.cloned.1.call-start
  8.1 1.1 compare_select_fusion
  9.2 0.0 copy-done
  9.2 0.0 copy-start.2
  9.2 0.9 convolution_bitcast_fusion
  10.1 0.0 all-reduce.3.cloned.1.call-update
  10.2 0.0 all-gather.2.cloned.1.call-start
  10.2 1.8 convolution_convert_fusion
  12.0 0.0 all-gather.2.cloned.1.call-update
  12.0 0.0 all-reduce.5.cloned.1.call-start
  12.1 0.0 copy-done.3
  12.1 0.1 copy.25
  12.2 0.0 copy-done.4
  12.2 0.0 copy-done.7
  12.2 0.0 copy-done.5
  12.3 0.0 copy-done.6
  12.3 20.5 %all-reduce.3.cloned.1.call-done = f32[256,256]{0,1:T(8,128)} async-done(((f32[256,256]{0,1:T(8,128)}), f32[256,256]{0,1:T(8,128)}) %all-reduce.3.cloned.1.call-update) | async-done | bytes 262160 | tf_op jit(solution)/shard_map/psum | solution.py:56
  32.8 0.0 all-reduce.5.cloned.1.call-update
  32.8 0.0 reduce-scatter.2.cloned.1.call-start
  32.9 44.9 %all-gather.2.cloned.1.call-done = bf16[4096,256]{1,0:T(8,128)(2,1)} async-done(((bf16[256,256]{1,0:T(8,128)(2,1)}), bf16[4096,256]{1,0:T(8,128)(2,1)}) %all-gather.2.cloned.1.call-update) | async-done | bytes 2097168 | tf_op jit(solution)/shard_map/all_gather | solution.py:45
  77.8 2.2 %gather_fusion.1 = bf16[16,128,256]{2,1,0:T(8,128)(2,1)S(1)} fusion(bf16[16,2,128,256]{3,2,1,0:T(8,128)(2,1)} %bitcast.44, s32[16]{0:T(128)S(1)} %get-tuple-element.9), kind=kCustom, calls=%fused_computation.1 | custom fusion | bytes 2097280 | tf_op jit(solution)/shard_map/gather | solution.py:14
  80.0 0.0 copy-done.2
  80.0 3.2 %gather_fusion = bf16[16,128,256]{2,1,0:T(8,128)(2,1)} fusion(bf16[16,2,128,256]{3,2,1,0:T(8,128)(2,1)} %bitcast.45, s32[16]{0:T(128)S(1)} %get-tuple-element.10), kind=kCustom, calls=%fused_computation | custom fusion | bytes 2097280 | tf_op jit(solution)/shard_map/gather | solution.py:14
  83.2 0.0 copy-start.1
  83.2 1.8 multiply_bitcast_fusion
  85.0 0.0 copy-done.1
  85.0 0.5 multiply_bitcast_fusion.1
  85.6 1.8 copy.18
  87.4 1.9 copy.20
  89.4 3.5 %scatter_fusion = f32[4,128,256]{2,1,0:T(8,128)S(1)} fusion(f32[4,128,256]{2,1,0:T(8,128)S(1)} %broadcast_in_dim.10, s32[16]{0:T(128)S(1)} %get-tuple-element.12, f32[16,128,256]{2,1,0:T(8,128)} %copy.18), kind=kCustom, calls=%fused_computation.3 | custom fusion | flops 524288 | bytes 6291520 | tf_op jit(solution)/shard_map/scatter-add | solution.py:19
  92.8 2.2 %scatter_fusion.1 = f32[4,128,256]{2,1,0:T(8,128)S(1)} fusion(f32[4,128,256]{2,1,0:T(8,128)S(1)} %scatter_fusion, s32[16]{0:T(128)S(1)} %get-tuple-element.11, f32[16,128,256]{2,1,0:T(8,128)S(1)} %copy.20), kind=kCustom, calls=%fused_computation.4 | custom fusion | flops 524288 | bytes 6291520 | tf_op jit(solution)/shard_map/scatter-add | solution.py:19
  95.0 1.6 gather_fusion.2
  96.6 0.9 broadcast_select_fusion
  97.6 0.0 reduce-scatter.2.cloned.1.call-update
  97.6 90.3 %all-reduce.5.cloned.1.call-done = f32[256,256]{0,1:T(8,128)} async-done(((f32[256,256]{0,1:T(8,128)}), f32[256,256]{0,1:T(8,128)}) %all-reduce.5.cloned.1.call-update) | async-done | bytes 262160 | tf_op jit(solution)/shard_map/psum | solution.py:57
  187.9 1.8 copy.21
  189.7 0.0 reduce-scatter.2.cloned.1.call-done
  189.7 1.6 convert_element_type.31
  (7 shorter events, 0.1 us)
Async XLA Ops:
  8.0 1.2 copy-start
  8.0 4.1 %copy-start.3 = (bf16[1,1,16,2,128,128]{5,4,3,2,1,0:T(8,128)(2,1)S(1)}, bf16[1,1,16,2,128,128]{5,4,3,2,1,0:T(8,128)(2,1)}, u32[]{:S(2)}) copy-start(bf16[1,1,16,2,128,128]{5,4,3,2,1,0:T(8,128)(2,1)} %param.13) | copy-start | bytes 3145732
  8.0 4.2 %copy-start.4 = (s32[1,512]{1,0:T(1,128)S(1)}, s32[1,512]{1,0:T(1,128)}, u32[]{:S(2)}) copy-start(s32[1,512]{1,0:T(1,128)} %param.17) | copy-start | bytes 6148
  8.0 4.2 %copy-start.7 = (s32[1,1,16]{2,1,0:T(1,128)S(1)}, s32[1,1,16]{2,1,0:T(1,128)}, u32[]{:S(2)}) copy-start(s32[1,1,16]{2,1,0:T(1,128)} %param.16) | copy-start | bytes 196
  8.0 4.2 %copy-start.5 = (s32[1,1,16,2]{2,3,1,0:T(2,128)S(1)}, s32[1,1,16,2]{2,3,1,0:T(2,128)}, u32[]{:S(2)}) copy-start(s32[1,1,16,2]{2,3,1,0:T(2,128)} %param.14) | copy-start | bytes 388
  8.1 4.2 %copy-start.6 = (s32[1,1,16,2]{2,3,1,0:T(2,128)S(1)}, s32[1,1,16,2]{2,3,1,0:T(2,128)}, u32[]{:S(2)}) copy-start(s32[1,1,16,2]{2,3,1,0:T(2,128)} %param.15) | copy-start | bytes 388
  8.1 24.7 %all-reduce.3.cloned.1.call-start = ((), (), s32[]{:S(2)}) async-start(), calls=%async_computation.3 | async-start | bytes 524288 | tf_op jit(solution)/shard_map/psum | solution.py:56
  9.2 70.8 %copy-start.2 = (bf16[256,256]{1,0:T(8,128)(2,1)}, bf16[256,256]{1,0:T(8,128)(2,1)S(1)}, u32[]{:S(2)}) copy-start(bf16[256,256]{1,0:T(8,128)(2,1)S(1)} %compare_select_fusion) | copy-start | bytes 393220
  10.2 67.6 %all-gather.2.cloned.1.call-start = ((), (), s32[]{:S(2)}) async-start(), calls=%async_computation.1 | async-start | bytes 2228224 | tf_op jit(solution)/shard_map/all_gather | solution.py:45
  12.0 175.9 %all-reduce.5.cloned.1.call-start = ((), (), s32[]{:S(2)}) async-start(), calls=%async_computation.4 | async-start | bytes 524288 | tf_op jit(solution)/shard_map/psum | solution.py:57
  32.8 156.8 %reduce-scatter.2.cloned.1.call-start = ((), (), s32[]{:S(2)}) async-start(), calls=%async_computation.2 | async-start | bytes 786432 | tf_op jit(solution)/shard_map/reduce_scatter | solution.py:53
  83.2 1.9 copy-start.1
Sparse Core Ops, SparseCore 0:
  11.8 20.9 all-reduce.2
  97.7 6.7 reduce-scatter.1
Sparse Core Ops, SparseCore 1:
  14.4 63.3 all-gather.1
  82.9 105.0 all-reduce.4
